TPU v7x, 512 devices: a whole 4x4x16 slice. The times are simulated.
512 devices in a mesh: pulse: 64 (over z, x), range: 8 (over y, core).
Axes of the slice: x: 4, y: 4, z: 16, core: 2. Of those that a mesh axis runs over, the one named last changes fastest.
Arguments:
- echo: bfloat16 [128, 2, 32768], P('pulse', None, 'range'), may hold values from -6 to 6
- chirp_phase: float32 [256], replicated, may hold values from -0.5 to 201.5624
- rec_phase: float32 [8, 8192, 2], P('range', 'pulse'), may hold values from -3.140625 to 3.140625
- rec_start: int32 [8, 8192], P('range', 'pulse'), may hold values from 0 to 32256
- rec_owner: int32 [8, 8192, 1], P('range', 'pulse'), may hold values from 0 to 511; in each aligned block of 128 rows (0 to 127, 128 to 255, ..., all dimensions but the last counted through in order) at most 2 rows name the same one
- rec_row: int32 [8, 8192], P('range', 'pulse'), may hold values from 0 to 63
- rec_weight: float32 [8, 8192], P('range', 'pulse'), may hold values from 0.2 to 1
- rec_count: int32 [8, 64], P('range', 'pulse'), may hold values from 96 to 128, as said below
- prior: bfloat16 [2048, 2, 4096], P('pulse', None, 'range'), may hold values from -6 to 6
- interp_weight: bfloat16 [64, 32], replicated, may hold values from -1 to 1
Outputs:
- tiles: float32 [4096, 2, 4096], P('pulse', None, 'range')
Inputs may be any that keep to these rules, and one draw needn't show every extreme that they name: `rec_owner`: in each aligned block of 128 record slots (one device's slots) no owner is named more than 2 times. Owner o is the tile of pulse index o // 8 and range index o % 8, 8 being the number of range devices. `rec_count`: some subimage has all 128 slots live.
All inputs are finite; a program needn't handle non-finite values.
Results may differ from a plain program's by a relative error of at most 0.0034.
Values may be sent and summed in bfloat16 or wider, within the bound.
A program may use at most 64 MiB of HBM per device.

v0:
```python
import jax
import jax.numpy as jnp
from jax import lax
from jax.sharding import PartitionSpec as P

SEG = 512


def shifted(block, axis, distance):
    devices = range(lax.axis_size(axis))
    route = [(i - distance, i) for i in devices if i - distance in devices]
    return lax.ppermute(block, axis, route)


def chirp_matrix(chirp_phase):
    tap_count = chirp_phase.shape[0]
    tap_scale = 1.0 / jnp.sqrt(jnp.float32(tap_count))
    real_taps = jnp.cos(chirp_phase) * tap_scale
    imag_taps = jnp.sin(chirp_phase) * tap_scale

    def banded(values):
        padded = jnp.concatenate([values, jnp.zeros((tap_count + 1,), jnp.float32)])
        return (
            jnp.tile(padded, tap_count)[: 2 * tap_count * tap_count]
            .reshape(tap_count, 2 * tap_count)
            .T
        )

    real_band = banded(real_taps)
    imag_band = banded(imag_taps)
    upper = jnp.concatenate([real_band, -imag_band], axis=1)
    lower = jnp.concatenate([imag_band, real_band], axis=1)
    return jnp.concatenate([upper, lower], axis=0).astype(jnp.bfloat16)


def compress(echo_block, tail_rim, filter_matrix):
    pulses, planes, bin_count = echo_block.shape
    tap_count = filter_matrix.shape[1] // 2
    block_count = bin_count // tap_count
    extended = jnp.concatenate([echo_block, tail_rim], axis=2)
    left_half = extended[:, :, :bin_count].reshape(pulses, planes, block_count, tap_count)
    right_half = extended[:, :, tap_count:].reshape(pulses, planes, block_count, tap_count)
    windows = jnp.concatenate([left_half, right_half], axis=3)
    windows = windows.transpose(0, 2, 1, 3).reshape(pulses * block_count, 2 * planes * tap_count)
    filtered = jnp.dot(windows, filter_matrix, preferred_element_type=jnp.float32)
    filtered = filtered.reshape(pulses, block_count, planes, tap_count).transpose(0, 2, 1, 3)
    return filtered.reshape(pulses, planes, bin_count).astype(jnp.bfloat16)


def cut_windows(block_table, starts):
    block_total = block_table.shape[0]
    first_block = starts // SEG
    second_block = jnp.minimum(first_block + 1, block_total - 1)
    offsets = starts % SEG
    paired = jnp.concatenate([block_table[first_block], block_table[second_block]], axis=3)
    for bit_number in range((SEG - 1).bit_length()):
        step_size = 1 << bit_number
        moved = jnp.concatenate(
            [paired[..., step_size:], jnp.zeros(paired.shape[:-1] + (step_size,), paired.dtype)],
            axis=3,
        )
        chosen = (offsets // step_size % 2 == 1)[:, None, None, None]
        paired = jnp.where(chosen, moved, paired)
    return paired[..., :SEG]


def form_records(block_table, starts, phases, scales):
    windows = cut_windows(block_table, starts)
    cosine = jnp.cos(phases).astype(jnp.bfloat16)
    sine_part = jnp.sin(phases).astype(jnp.bfloat16)
    real_part = windows[:, :, 0]
    imag_part = windows[:, :, 1]
    out_real = jnp.einsum(
        "bk,bks->bs", cosine, real_part, preferred_element_type=jnp.float32
    ) - jnp.einsum("bk,bks->bs", sine_part, imag_part, preferred_element_type=jnp.float32)
    out_imag = jnp.einsum(
        "bk,bks->bs", cosine, imag_part, preferred_element_type=jnp.float32
    ) + jnp.einsum("bk,bks->bs", sine_part, real_part, preferred_element_type=jnp.float32)
    return (jnp.stack([out_real, out_imag], axis=1) * scales[:, None, None]).astype(jnp.bfloat16)


def on_device(
    echo,
    chirp_phase,
    rec_phase,
    rec_start,
    rec_owner,
    rec_row,
    rec_weight,
    rec_count,
    prior,
    interp_weight,
):
    filter_matrix = chirp_matrix(chirp_phase)
    tap_count = chirp_phase.shape[0]
    tail_rim = shifted(echo[:, :, :tap_count], "range", -1)
    profiles = lax.all_gather(compress(echo, tail_rim, filter_matrix), "range", axis=2, tiled=True)
    pulses, planes, bin_total = profiles.shape
    block_table = profiles.reshape(pulses, planes, bin_total // SEG, SEG).transpose(2, 0, 1, 3)
    slot_count = rec_start.shape[1]
    starts = rec_start[0]
    phases = rec_phase[0]
    owners = rec_owner[0, :, 0]
    dest_rows = rec_row[0]
    weights = rec_weight[0]
    live_mask = (jnp.arange(slot_count) < rec_count[0, 0]).astype(jnp.float32)
    scales = live_mask * weights / jnp.sqrt(jnp.float32(pulses))
    block_size = min(64, slot_count)
    group_count = slot_count // block_size

    def form_group(items):
        return form_records(block_table, items[0], items[1], items[2])

    records = lax.map(
        form_group,
        (
            starts.reshape(group_count, block_size),
            phases.reshape(group_count, block_size, pulses),
            scales.reshape(group_count, block_size),
        ),
    )
    records = records.reshape(slot_count, 2 * SEG)
    pulse_count = lax.axis_size("pulse")
    range_count = lax.axis_size("range")
    owner_total = pulse_count * range_count
    capacity = max(2, 3 * slot_count // (2 * owner_total))
    owner_marks = (owners[:, None] == jnp.arange(owner_total)[None, :]).astype(jnp.int32)
    earlier = jnp.cumsum(owner_marks, axis=0) - owner_marks
    slot_rank = jnp.sum(earlier * owner_marks, axis=1)
    slot_index = owners * capacity + slot_rank
    placement = slot_index[None, :] == jnp.arange(owner_total * capacity)[:, None]
    outgoing = jnp.dot(
        placement.astype(jnp.bfloat16), records, preferred_element_type=jnp.float32
    ).astype(jnp.bfloat16)
    row_slots = jnp.sum(placement.astype(jnp.int32) * dest_rows[None, :], axis=1)
    outgoing = outgoing.reshape(pulse_count, range_count, capacity, 2, SEG)
    row_slots = row_slots.reshape(pulse_count, range_count, capacity)
    incoming, incoming_rows = (
        lax.all_to_all(
            lax.all_to_all(outgoing, "pulse", split_axis=0, concat_axis=0, tiled=True),
            "range",
            split_axis=1,
            concat_axis=1,
            tiled=True,
        ),
        lax.all_to_all(
            lax.all_to_all(row_slots, "pulse", split_axis=0, concat_axis=0, tiled=True),
            "range",
            split_axis=1,
            concat_axis=1,
            tiled=True,
        ),
    )
    incoming = incoming.reshape(-1, 2, SEG)
    incoming_rows = incoming_rows.reshape(-1)
    out_rows = interp_weight.shape[0]
    tile_image = jnp.einsum("rm,mcs->rcs", interp_weight, prior, preferred_element_type=jnp.float32)
    row_table = (incoming_rows[:, None] == jnp.arange(out_rows)[None, :]).astype(jnp.bfloat16)
    tile_image = tile_image + jnp.einsum(
        "jr,jcs->rcs", row_table, incoming, preferred_element_type=jnp.float32
    )
    return tile_image


def solution(mesh):
    placed = (
        P("pulse", None, "range"),
        P(),
        P("range", "pulse", None),
        P("range", "pulse"),
        P("range", "pulse", None),
        P("range", "pulse"),
        P("range", "pulse"),
        P("range", "pulse"),
        P("pulse", None, "range"),
        P(),
    )
    return jax.shard_map(
        on_device, mesh=mesh, in_specs=placed, out_specs=P("pulse", None, "range"), check_vma=False
    )
```

profile of v0, /device:TPU:1, one launch (start us, length us, event | category | flops | bytes accessed | tf_op | source)
XLA Modules:
  0.0 257.0 jit_solution(12730651310429651620)
XLA Ops:
  0.7 8.8 %collective-permute-start = (bf16[2,2,256]{2,1,0:T(2,128)(2,1)S(1)}, bf16[2,2,256]{2,1,0:T(2,128)(2,1)S(1)}, u32[]{:S(2)}, u32[]{:S(2)}) collective-permute-start(bf16[2,2,256]{2,1,0:T(2,128)(2,1)S(1)} %slice.92), channel_id=1, source_target_pairs={{1,0},{2,1},{3,2},{4,3},{5,4},{6,5},{7,6},{9,8},{10,9},{11,10},{12... | collective-permute-start | bytes 6152 | tf_op jit(solution)/shard_map/ppermute | solution.py:12
  13.1 1.1 copy.61
  14.2 12.9 %all-to-all-start = ((s32[64,8,2]{1,2,0:T(2,128)}), s32[64,8,2]{1,2,0:T(2,128)S(1)}, u32[]{:S(2)}, u32[]{:S(2)}) async-start(s32[64,8,2]{1,2,0:T(2,128)} %copy.61), calls=%async_computation | async-start | bytes 131072 | tf_op jit(solution)/shard_map/all_to_all | solution.py:147
  33.8 13.5 %all_gather.3 = bf16[2,2,32768]{2,1,0:T(2,128)(2,1)S(1)} all-gather(bf16[2,2,4096]{2,1,0:T(2,128)(2,1)S(1)} %convert_element_type.57), channel_id=1, replica_groups=mesh['pulse'=64,'range'=8] {'range'}, dimensions={2}, use_global_device_ids=true | all-gather | bytes 294912 | tf_op jit(solution)/shard_map/all_gather | solution.py:97
  47.8 42.9 %while.13 = (s32[]{:T(128)}, bf16[2,64,2,512]{3,2,1,0:T(2,128)(2,1)S(1)}, f32[2,64,2]{1,0,2:T(2,128)S(1)}, s32[2,64]{1,0:T(2,128)S(1)}, bf16[64,2,2,512]{3,2,1,0...) while((s32[]{:T(128)}, bf16[2,64,2,512]{3,2,1,0:T(2,128)(2,1)S(1)}, f32[2,64,2]{1,0,2:T(2,128)S(1)}, ...), condition=%wide.region_4.5_spmd, body=%wide.region_3.4_spmd.sunk | while | flops 3162434 | bytes 28723936 | solution.py:114
  48.0 1.1 gather_fusion
  49.3 1.1 gather_fusion.1
  50.6 1.0 slice.137
  52.7 1.0 slice.138
  54.7 1.0 slice.139
  56.7 1.0 slice.140
  58.7 1.0 slice.141
  60.7 1.0 slice.142
  62.7 1.0 slice.143
  69.3 1.1 gather_fusion
  70.5 1.1 gather_fusion.1
  73.9 1.0 slice.138
  75.9 1.0 slice.139
  77.9 1.0 slice.140
  79.9 1.0 slice.141
  81.9 1.0 slice.142
  83.9 1.0 slice.143
  91.4 2.7 %reshape.460 = bf16[64,8,2,2,512]{4,3,2,1,0:T(2,128)(2,1)} reshape(bf16[1024,1024]{1,0:T(8,128)(2,1)S(1)} %convolution_convert_fusion) | data formatting | bytes 4194304 | tf_op jit(solution)/shard_map/reshape | solution.py:136
  94.1 14.8 %all-to-all-start.2 = ((bf16[64,8,2,2,512]{4,3,2,1,0:T(2,128)(2,1)}), bf16[64,8,2,2,512]{4,3,2,1,0:T(2,128)(2,1)S(1)}, u32[]{:S(2)}, u32[]{:S(2)}) async-start(bf16[64,8,2,2,512]{4,3,2,1,0:T(2,128)(2,1)} %reshape.460), calls=%async_computation.2 | async-start | bytes 4194304 | tf_op jit(solution)/shard_map/all_to_all | solution.py:140
  109.7 96.3 %all-to-all-done.2 = bf16[64,8,2,2,512]{4,3,2,1,0:T(2,128)(2,1)S(1)} async-done(((bf16[64,8,2,2,512]{4,3,2,1,0:T(2,128)(2,1)}), bf16[64,8,2,2,512]{4,3,2,1,0:T(2,128)(2,1)S(1)}, u32[]{:S(2)}, u32[]{:S(2)}) %all-to-all-start.2) | async-done | bytes 2097184 | tf_op jit(solution)/shard_map/all_to_all | solution.py:140
  206.0 8.1 %all-to-all-start.1 = ((s32[8,1,128]{2,1,0:T(1,128)}), s32[8,1,128]{2,1,0:T(1,128)S(1)}, u32[]{:S(2)}, u32[]{:S(2)}) async-start(s32[8,1,128]{2,1,0:T(1,128)} %reshape.511), calls=%async_computation.1 | async-start | bytes 8192 | tf_op jit(solution)/shard_map/all_to_all | solution.py:146
  214.1 3.0 %copy.68 = bf16[64,8,2,2,512]{4,3,2,0,1:T(2,128)(2,1)} copy(bf16[64,8,2,2,512]{4,3,2,1,0:T(2,128)(2,1)S(1)} %all-to-all-done.2) | data formatting | bytes 4194304 | tf_op jit(solution)/shard_map/all_to_all | solution.py:140
  217.0 1.5 all-to-all-done.1
  218.6 4.2 %all-to-all-start.3 = ((bf16[64,8,2,2,512]{4,3,2,0,1:T(2,128)(2,1)}), bf16[64,8,2,2,512]{4,3,2,0,1:T(2,128)(2,1)S(1)}, u32[]{:S(2)}, u32[]{:S(2)}) async-start(bf16[64,8,2,2,512]{4,3,2,0,1:T(2,128)(2,1)} %copy.68), calls=%async_computation.3 | async-start | bytes 4194304 | tf_op jit(solution)/shard_map/all_to_all | solution.py:139
  224.6 24.5 %all-to-all-done.3 = bf16[64,8,2,2,512]{4,3,2,0,1:T(2,128)(2,1)S(1)} async-done(((bf16[64,8,2,2,512]{4,3,2,0,1:T(2,128)(2,1)}), bf16[64,8,2,2,512]{4,3,2,0,1:T(2,128)(2,1)S(1)}, u32[]{:S(2)}, u32[]{:S(2)}) %all-to-all-start.3) | async-done | bytes 2097184 | tf_op jit(solution)/shard_map/all_to_all | solution.py:139
  249.1 3.8 %copy.69 = bf16[64,8,2,2,512]{4,2,1,0,3:T(2,128)(2,1)} copy(bf16[64,8,2,2,512]{4,3,2,0,1:T(2,128)(2,1)S(1)} %all-to-all-done.3) | data formatting | bytes 4194304 | tf_op jit(solution)/shard_map/all_to_all | solution.py:139
  252.9 2.7 %reshape.461 = bf16[1024,2,512]{2,0,1:T(8,128)(2,1)S(1)} reshape(bf16[64,8,2,2,512]{4,2,1,0,3:T(2,128)(2,1)} %copy.69) | data formatting | bytes 4194304 | tf_op jit(solution)/shard_map/reshape | solution.py:154
  (137 shorter events, 39.7 us)
Async XLA Ops:
  0.0 222.8 %copy-start = (bf16[32,2,512]{2,1,0:T(2,128)(2,1)S(1)}, bf16[32,2,512]{2,1,0:T(2,128)(2,1)}, u32[]{:S(2)}) copy-start(bf16[32,2,512]{2,1,0:T(2,128)(2,1)} %param.20) | copy-start | bytes 196612
  0.7 32.5 %collective-permute-start = (bf16[2,2,256]{2,1,0:T(2,128)(2,1)S(1)}, bf16[2,2,256]{2,1,0:T(2,128)(2,1)S(1)}, u32[]{:S(2)}, u32[]{:S(2)}) collective-permute-start(bf16[2,2,256]{2,1,0:T(2,128)(2,1)S(1)} %slice.92), channel_id=1, source_target_pairs={{1,0},{2,1},{3,2},{4,3},{5,4},{6,5},{7,6},{9,8},{10,9},{11,10},{12... | collective-permute-start | bytes 6152 | tf_op jit(solution)/shard_map/ppermute | solution.py:12
  10.5 18.0 %copy-start.4 = (f32[256]{0:T(256)S(1)}, f32[256]{0:T(256)}, u32[]{:S(2)}) copy-start(f32[256]{0:T(256)} %param.13) | copy-start | bytes 3076
  14.2 80.0 %all-to-all-start = ((s32[64,8,2]{1,2,0:T(2,128)}), s32[64,8,2]{1,2,0:T(2,128)S(1)}, u32[]{:S(2)}, u32[]{:S(2)}) async-start(s32[64,8,2]{1,2,0:T(2,128)} %copy.61), calls=%async_computation | async-start | bytes 131072 | tf_op jit(solution)/shard_map/all_to_all | solution.py:147
  28.4 1.9 copy-start.5
  28.7 3.1 %copy-start.3 = (f32[1,128,2]{1,2,0:T(2,128)S(1)}, f32[1,128,2]{1,2,0:T(2,128)}, u32[]{:S(2)}) copy-start(f32[1,128,2]{1,2,0:T(2,128)} %param.14) | copy-start | bytes 3076
  28.7 3.7 %copy-start.6 = (s32[1,128]{1,0:T(1,128)S(1)}, s32[1,128]{1,0:T(1,128)}, u32[]{:S(2)}) copy-start(s32[1,128]{1,0:T(1,128)} %param.15) | copy-start | bytes 1540
  28.7 4.5 %copy-start.1 = (bf16[2,2,4096]{2,1,0:T(2,128)(2,1)S(1)}, bf16[2,2,4096]{2,1,0:T(2,128)(2,1)}, u32[]{:S(2)}) copy-start(bf16[2,2,4096]{2,1,0:T(2,128)(2,1)} %param.12) | copy-start | bytes 98308
  94.1 111.8 %all-to-all-start.2 = ((bf16[64,8,2,2,512]{4,3,2,1,0:T(2,128)(2,1)}), bf16[64,8,2,2,512]{4,3,2,1,0:T(2,128)(2,1)S(1)}, u32[]{:S(2)}, u32[]{:S(2)}) async-start(bf16[64,8,2,2,512]{4,3,2,1,0:T(2,128)(2,1)} %reshape.460), calls=%async_computation.2 | async-start | bytes 4194304 | tf_op jit(solution)/shard_map/all_to_all | solution.py:140
  206.0 12.6 %all-to-all-start.1 = ((s32[8,1,128]{2,1,0:T(1,128)}), s32[8,1,128]{2,1,0:T(1,128)S(1)}, u32[]{:S(2)}, u32[]{:S(2)}) async-start(s32[8,1,128]{2,1,0:T(1,128)} %reshape.511), calls=%async_computation.1 | async-start | bytes 8192 | tf_op jit(solution)/shard_map/all_to_all | solution.py:146
  217.0 5.7 %copy-start.2 = (bf16[64,32]{0,1:T(8,128)(2,1)S(1)}, bf16[64,32]{0,1:T(8,128)(2,1)}, u32[]{:S(2)}) copy-start(bf16[64,32]{0,1:T(8,128)(2,1)} %param.21) | copy-start | bytes 12292
  218.6 30.6 %all-to-all-start.3 = ((bf16[64,8,2,2,512]{4,3,2,0,1:T(2,128)(2,1)}), bf16[64,8,2,2,512]{4,3,2,0,1:T(2,128)(2,1)S(1)}, u32[]{:S(2)}, u32[]{:S(2)}) async-start(bf16[64,8,2,2,512]{4,3,2,0,1:T(2,128)(2,1)} %copy.68), calls=%async_computation.3 | async-start | bytes 4194304 | tf_op jit(solution)/shard_map/all_to_all | solution.py:139
where the time goes:
time: 258 us; the launch traced here: 257 us
  waiting for transfers between devices  122 us (47%)
  starting transfers between devices  48.8 us (19%)
  local copies, waits for them, and re-layouts  42.8 us (17%)
  other arithmetic  23.8 us (9%)
  blocking collectives  13.5 us (5%)
  matrix products  3.96 us (2%)
    all_to_all x1, waiting for transfers between devices, on_device(): lax.all_to_all(outgoing, 'pulse', split_axis=0, concat_axis=0, tiled=True)  96.3 us
    all_to_all x1, waiting for transfers between devices, on_device(): lax.all_to_all(lax.all_to_all(outgoing, 'pulse', split_axis=0, concat_axi...  24.5 us
    select_n x18, other arithmetic, cut_windows(): paired = jnp.where(chosen, moved, paired)  16.4 us
    slice x18, local copies, waits for them, and re-layouts, cut_windows(): paired[..., step_size:]  15.4 us
    all_to_all x1, starting transfers between devices, on_device(): lax.all_to_all(outgoing, 'pulse', split_axis=0, concat_axis=0, tiled=True)  14.8 us
    all_gather x1, blocking collectives, on_device(): lax.all_gather(compress(echo, tail_rim, filter_matrix), 'range', axis=2,...  13.5 us
    all_to_all x1, starting transfers between devices, on_device(): lax.all_to_all(row_slots, 'pulse', split_axis=0, concat_axis=0, tiled=True)  12.9 us
    ppermute x1, starting transfers between devices, shifted(): return lax.ppermute(block, axis, route)  8.77 us
  transfers between devices with their start and end apart: 5, of which 3 were waited for; matrix products, arithmetic and copies ran while one was open for 24% of the time, Pallas kernels for 0%

commit v1 on v0

--- a/solution.py
+++ b/solution.py
@@ -91,10 +91,22 @@
     prior,
     interp_weight,
 ):
+
+    def switch_turns(arr_in, which_dim):
+        return jnp.concatenate(
+            lax.all_to_all(
+                jnp.stack(tuple((arr_in for _ in range(lax.axis_size("range"))))),
+                axis_name="range",
+                split_axis=0,
+                concat_axis=0,
+            ),
+            which_dim,
+        )
+
     filter_matrix = chirp_matrix(chirp_phase)
     tap_count = chirp_phase.shape[0]
     tail_rim = shifted(echo[:, :, :tap_count], "range", -1)
-    profiles = lax.all_gather(compress(echo, tail_rim, filter_matrix), "range", axis=2, tiled=True)
+    profiles = switch_turns(compress(echo, tail_rim, filter_matrix), 2)
     pulses, planes, bin_total = profiles.shape
     block_table = profiles.reshape(pulses, planes, bin_total // SEG, SEG).transpose(2, 0, 1, 3)
     slot_count = rec_start.shape[1]

time: 258 us -> 248 us (0.961)
  blocking collectives: 13.5 us -> 0 us
  starting transfers between devices: 48.8 us -> 56.3 us
  other arithmetic: 23.8 us -> 21.2 us
    all_gather x1 -> x0, blocking collectives: 13.5 us -> none  [on_device(): lax.all_gather(compress(echo, tail_rim, filter_matrix), 'range', axis=2,...]
    all_to_all x0 -> x1, starting transfers between devices: none -> 3.36 us  [switch_turns(): lax.all_to_all(jnp.stack(tuple((arr_in for _ in range(lax.axis_size('rang...]
    all_to_all x1, waiting for transfers between devices: 96.3 us -> 93 us  [on_device(): lax.all_to_all(outgoing, 'pulse', split_axis=0, concat_axis=0, tiled=True)]
    all_to_all x1, starting transfers between devices: 8.09 us -> 10.7 us  [on_device(): lax.all_to_all(lax.all_to_all(row_slots, 'pulse', split_axis=0, concat_ax...]
  transfers between devices with their start and end apart: 5 -> 6, of which waited for: 3 -> 4; matrix products, arithmetic and copies ran while one was open for 24% -> 24% of each run, Pallas kernels for 0% -> 0%
where the time goes in v1:
time: 248 us; the launch traced here: 247 us
  waiting for transfers between devices  120 us (48%)
  starting transfers between devices  56.3 us (23%)
  local copies, waits for them, and re-layouts  43.9 us (18%)
  other arithmetic  21.2 us (9%)
  matrix products  3.97 us (2%)
    all_to_all x1, waiting for transfers between devices, on_device(): lax.all_to_all(outgoing, 'pulse', split_axis=0, concat_axis=0, tiled=True)  93 us
    all_to_all x1, waiting for transfers between devices, on_device(): lax.all_to_all(lax.all_to_all(outgoing, 'pulse', split_axis=0, concat_axi...  24.5 us
    select_n x18, other arithmetic, cut_windows(): paired = jnp.where(chosen, moved, paired)  16.4 us
    slice x18, local copies, waits for them, and re-layouts, cut_windows(): paired[..., step_size:]  15.4 us
    all_to_all x1, starting transfers between devices, on_device(): lax.all_to_all(row_slots, 'pulse', split_axis=0, concat_axis=0, tiled=True)  14.8 us
    all_to_all x1, starting transfers between devices, on_device(): lax.all_to_all(outgoing, 'pulse', split_axis=0, concat_axis=0, tiled=True)  14.5 us
    all_to_all x1, starting transfers between devices, on_device(): lax.all_to_all(lax.all_to_all(row_slots, 'pulse', split_axis=0, concat_ax...  10.7 us
    ppermute x1, starting transfers between devices, shifted(): return lax.ppermute(block, axis, route)  8.77 us
  transfers between devices with their start and end apart: 6, of which 4 were waited for; matrix products, arithmetic and copies ran while one was open for 24% of the time, Pallas kernels for 0%

profile of v1, /device:TPU:1, one launch (start us, length us, event | category | flops | bytes accessed | tf_op | source)
XLA Modules:
  0.0 247.3 jit_solution(6578514160226730536)
XLA Ops:
  0.7 8.8 %collective-permute-start = (bf16[2,2,256]{2,1,0:T(2,128)(2,1)S(1)}, bf16[2,2,256]{2,1,0:T(2,128)(2,1)S(1)}, u32[]{:S(2)}, u32[]{:S(2)}) collective-permute-start(bf16[2,2,256]{2,1,0:T(2,128)(2,1)S(1)} %slice.92), channel_id=1, source_target_pairs={{1,0},{2,1},{3,2},{4,3},{5,4},{6,5},{7,6},{9,8},{10,9},{11,10},{12... | collective-permute-start | bytes 6152 | tf_op jit(solution)/shard_map/ppermute | solution.py:12
  14.4 3.4 %all-to-all-start.2 = ((bf16[8,2,2,4096]{3,2,1,0:T(2,128)(2,1)}), bf16[8,2,2,4096]{3,2,1,0:T(2,128)(2,1)S(1)}, u32[]{:S(2)}, u32[]{:S(2)}) async-start(bf16[8,2,2,4096]{3,2,1,0:T(2,128)(2,1)} %stack.8), calls=%async_computation.2 | async-start | bytes 524288 | tf_op jit(solution)/shard_map/all_to_all | solution.py:97
  21.6 1.1 copy.63
  22.6 1.0 all-to-all-done.2
  23.6 14.8 %all-to-all-start = ((s32[64,8,2]{1,2,0:T(2,128)}), s32[64,8,2]{1,2,0:T(2,128)S(1)}, u32[]{:S(2)}, u32[]{:S(2)}) async-start(s32[64,8,2]{1,2,0:T(2,128)} %copy.63), calls=%async_computation | async-start | bytes 131072 | tf_op jit(solution)/shard_map/all_to_all | solution.py:159
  39.0 42.9 %while.13 = (s32[]{:T(128)}, bf16[2,64,2,512]{3,2,1,0:T(2,128)(2,1)S(1)}, f32[2,64,2]{1,0,2:T(2,128)S(1)}, s32[2,64]{1,0:T(2,128)S(1)}, bf16[64,2,2,512]{3,2,1,0...) while((s32[]{:T(128)}, bf16[2,64,2,512]{3,2,1,0:T(2,128)(2,1)S(1)}, f32[2,64,2]{1,0,2:T(2,128)S(1)}, ...), condition=%wide.region_4.5_spmd, body=%wide.region_3.4_spmd.sunk | while | flops 3162434 | bytes 28723936 | solution.py:126
  39.2 1.1 gather_fusion
  40.5 1.1 gather_fusion.1
  43.9 1.0 slice.138
  45.9 1.0 slice.139
  47.9 1.0 slice.140
  49.9 1.0 slice.141
  51.9 1.0 slice.142
  53.9 1.0 slice.143
  60.5 1.1 gather_fusion
  61.8 1.1 gather_fusion.1
  65.1 1.0 slice.138
  67.1 1.0 slice.139
  69.1 1.0 slice.140
  71.1 1.0 slice.141
  73.1 1.0 slice.142
  75.1 1.0 slice.143
  82.6 2.8 %reshape.463 = bf16[64,8,2,2,512]{4,3,2,1,0:T(2,128)(2,1)} reshape(bf16[1024,1024]{1,0:T(8,128)(2,1)S(1)} %convolution_convert_fusion) | data formatting | bytes 4194304 | tf_op jit(solution)/shard_map/reshape | solution.py:148
  85.4 14.5 %all-to-all-start.3 = ((bf16[64,8,2,2,512]{4,3,2,1,0:T(2,128)(2,1)}), bf16[64,8,2,2,512]{4,3,2,1,0:T(2,128)(2,1)S(1)}, u32[]{:S(2)}, u32[]{:S(2)}) async-start(bf16[64,8,2,2,512]{4,3,2,1,0:T(2,128)(2,1)} %reshape.463), calls=%async_computation.3 | async-start | bytes 4194304 | tf_op jit(solution)/shard_map/all_to_all | solution.py:152
  100.7 93.0 %all-to-all-done.3 = bf16[64,8,2,2,512]{4,3,2,1,0:T(2,128)(2,1)S(1)} async-done(((bf16[64,8,2,2,512]{4,3,2,1,0:T(2,128)(2,1)}), bf16[64,8,2,2,512]{4,3,2,1,0:T(2,128)(2,1)S(1)}, u32[]{:S(2)}, u32[]{:S(2)}) %all-to-all-start.3) | async-done | bytes 2097184 | tf_op jit(solution)/shard_map/all_to_all | solution.py:152
  193.6 10.7 %all-to-all-start.1 = ((s32[8,1,128]{2,1,0:T(1,128)}), s32[8,1,128]{2,1,0:T(1,128)S(1)}, u32[]{:S(2)}, u32[]{:S(2)}) async-start(s32[8,1,128]{2,1,0:T(1,128)} %reshape.514), calls=%async_computation.1 | async-start | bytes 8192 | tf_op jit(solution)/shard_map/all_to_all | solution.py:158
  204.3 3.0 %copy.71 = bf16[64,8,2,2,512]{4,3,2,0,1:T(2,128)(2,1)} copy(bf16[64,8,2,2,512]{4,3,2,1,0:T(2,128)(2,1)S(1)} %all-to-all-done.3) | data formatting | bytes 4194304 | tf_op jit(solution)/shard_map/all_to_all | solution.py:152
  207.3 1.6 all-to-all-done.1
  208.8 4.2 %all-to-all-start.4 = ((bf16[64,8,2,2,512]{4,3,2,0,1:T(2,128)(2,1)}), bf16[64,8,2,2,512]{4,3,2,0,1:T(2,128)(2,1)S(1)}, u32[]{:S(2)}, u32[]{:S(2)}) async-start(bf16[64,8,2,2,512]{4,3,2,0,1:T(2,128)(2,1)} %copy.71), calls=%async_computation.4 | async-start | bytes 4194304 | tf_op jit(solution)/shard_map/all_to_all | solution.py:151
  214.9 24.5 %all-to-all-done.4 = bf16[64,8,2,2,512]{4,3,2,0,1:T(2,128)(2,1)S(1)} async-done(((bf16[64,8,2,2,512]{4,3,2,0,1:T(2,128)(2,1)}), bf16[64,8,2,2,512]{4,3,2,0,1:T(2,128)(2,1)S(1)}, u32[]{:S(2)}, u32[]{:S(2)}) %all-to-all-start.4) | async-done | bytes 2097184 | tf_op jit(solution)/shard_map/all_to_all | solution.py:151
  239.4 3.8 %copy.72 = bf16[64,8,2,2,512]{4,2,1,0,3:T(2,128)(2,1)} copy(bf16[64,8,2,2,512]{4,3,2,0,1:T(2,128)(2,1)S(1)} %all-to-all-done.4) | data formatting | bytes 4194304 | tf_op jit(solution)/shard_map/all_to_all | solution.py:151
  243.1 2.7 %reshape.464 = bf16[1024,2,512]{2,0,1:T(8,128)(2,1)S(1)} reshape(bf16[64,8,2,2,512]{4,2,1,0,3:T(2,128)(2,1)} %copy.72) | data formatting | bytes 4194304 | tf_op jit(solution)/shard_map/reshape | solution.py:166
  (144 shorter events, 39.1 us)
Async XLA Ops:
  0.0 213.0 %copy-start = (bf16[32,2,512]{2,1,0:T(2,128)(2,1)S(1)}, bf16[32,2,512]{2,1,0:T(2,128)(2,1)}, u32[]{:S(2)}) copy-start(bf16[32,2,512]{2,1,0:T(2,128)(2,1)} %param.20) | copy-start | bytes 196612
  0.0 10.9 %copy-start.5 = (f32[256]{0:T(256)S(1)}, f32[256]{0:T(256)}, u32[]{:S(2)}) copy-start(f32[256]{0:T(256)} %param.13) | copy-start | bytes 3076
  0.0 10.9 %copy-start.3 = (s32[1,128,1]{1,2,0:T(1,128)S(1)}, s32[1,128,1]{1,2,0:T(1,128)}, u32[]{:S(2)}) copy-start(s32[1,128,1]{1,2,0:T(1,128)} %param.16) | copy-start | bytes 1540
  0.7 12.2 %collective-permute-start = (bf16[2,2,256]{2,1,0:T(2,128)(2,1)S(1)}, bf16[2,2,256]{2,1,0:T(2,128)(2,1)S(1)}, u32[]{:S(2)}, u32[]{:S(2)}) collective-permute-start(bf16[2,2,256]{2,1,0:T(2,128)(2,1)S(1)} %slice.92), channel_id=1, source_target_pairs={{1,0},{2,1},{3,2},{4,3},{5,4},{6,5},{7,6},{9,8},{10,9},{11,10},{12... | collective-permute-start | bytes 6152 | tf_op jit(solution)/shard_map/ppermute | solution.py:12
  11.7 1.2 copy-start.1
  12.7 5.1 %copy-start.6 = (s32[1,128]{1,0:T(1,128)S(1)}, s32[1,128]{1,0:T(1,128)}, u32[]{:S(2)}) copy-start(s32[1,128]{1,0:T(1,128)} %param.17) | copy-start | bytes 1540
  12.7 5.9 %copy-start.7 = (f32[1,128]{1,0:T(1,128)S(1)}, f32[1,128]{1,0:T(1,128)}, u32[]{:S(2)}) copy-start(f32[1,128]{1,0:T(1,128)} %param.18) | copy-start | bytes 1540
  12.7 7.2 %copy-start.4 = (f32[1,128,2]{1,2,0:T(2,128)S(1)}, f32[1,128,2]{1,2,0:T(2,128)}, u32[]{:S(2)}) copy-start(f32[1,128,2]{1,2,0:T(2,128)} %param.14) | copy-start | bytes 3076
  12.7 7.9 %copy-start.8 = (s32[1,128]{1,0:T(1,128)S(1)}, s32[1,128]{1,0:T(1,128)}, u32[]{:S(2)}) copy-start(s32[1,128]{1,0:T(1,128)} %param.15) | copy-start | bytes 1540
  14.4 9.2 %all-to-all-start.2 = ((bf16[8,2,2,4096]{3,2,1,0:T(2,128)(2,1)}), bf16[8,2,2,4096]{3,2,1,0:T(2,128)(2,1)S(1)}, u32[]{:S(2)}, u32[]{:S(2)}) async-start(bf16[8,2,2,4096]{3,2,1,0:T(2,128)(2,1)} %stack.8), calls=%async_computation.2 | async-start | bytes 524288 | tf_op jit(solution)/shard_map/all_to_all | solution.py:97
  23.6 61.7 %all-to-all-start = ((s32[64,8,2]{1,2,0:T(2,128)}), s32[64,8,2]{1,2,0:T(2,128)S(1)}, u32[]{:S(2)}, u32[]{:S(2)}) async-start(s32[64,8,2]{1,2,0:T(2,128)} %copy.63), calls=%async_computation | async-start | bytes 131072 | tf_op jit(solution)/shard_map/all_to_all | solution.py:159
  85.4 108.3 %all-to-all-start.3 = ((bf16[64,8,2,2,512]{4,3,2,1,0:T(2,128)(2,1)}), bf16[64,8,2,2,512]{4,3,2,1,0:T(2,128)(2,1)S(1)}, u32[]{:S(2)}, u32[]{:S(2)}) async-start(bf16[64,8,2,2,512]{4,3,2,1,0:T(2,128)(2,1)} %reshape.463), calls=%async_computation.3 | async-start | bytes 4194304 | tf_op jit(solution)/shard_map/all_to_all | solution.py:152
  193.6 15.2 %all-to-all-start.1 = ((s32[8,1,128]{2,1,0:T(1,128)}), s32[8,1,128]{2,1,0:T(1,128)S(1)}, u32[]{:S(2)}, u32[]{:S(2)}) async-start(s32[8,1,128]{2,1,0:T(1,128)} %reshape.514), calls=%async_computation.1 | async-start | bytes 8192 | tf_op jit(solution)/shard_map/all_to_all | solution.py:158
  207.3 5.8 %copy-start.2 = (bf16[64,32]{0,1:T(8,128)(2,1)S(1)}, bf16[64,32]{0,1:T(8,128)(2,1)}, u32[]{:S(2)}) copy-start(bf16[64,32]{0,1:T(8,128)(2,1)} %param.21) | copy-start | bytes 12292
  208.8 30.6 %all-to-all-start.4 = ((bf16[64,8,2,2,512]{4,3,2,0,1:T(2,128)(2,1)}), bf16[64,8,2,2,512]{4,3,2,0,1:T(2,128)(2,1)S(1)}, u32[]{:S(2)}, u32[]{:S(2)}) async-start(bf16[64,8,2,2,512]{4,3,2,0,1:T(2,128)(2,1)} %copy.71), calls=%async_computation.4 | async-start | bytes 4194304 | tf_op jit(solution)/shard_map/all_to_all | solution.py:151
